TPU v7x, 32 devices: a whole 2x2x4 slice. The times are simulated.
32 devices in a mesh: cd: 8 (over z, y), ab: 4 (over x, core).
Axes of the slice: x: 2, y: 2, z: 4, core: 2. Of those that a mesh axis runs over, the one named last changes fastest.
Arguments:
- amplitudes: bfloat16 [512, 8, 800], P('cd', None, 'ab'), may hold values from -6 to 6
- integrals: bfloat16 [8, 800, 2048], P('cd', None, 'ab'), may hold values from -0.078125 to 0.078125
Outputs:
- ladder: float32 [512, 2048], P('cd', 'ab')
All inputs are finite; a program needn't handle non-finite values.
Results may differ from a plain program's by a relative error of at most 0.0003.
Values may be sent and summed in bfloat16 or wider, within the bound.
A program may use at most 64 MiB of HBM per device.

v0:
```python
import functools

import jax
import jax.numpy as jnp
from jax import lax
from jax.experimental import pallas as pl
from jax.experimental.pallas import tpu as pltpu
from jax.sharding import PartitionSpec as P

MESH = pl.DeviceIdType.MESH
LANES = 128
ORDER = (5, 7, 3, 1, 4, 6, 2, 0)
DIRECT = ()
PLAN = (
    ("a", 5), ("r", 5), ("a", 7), ("p", 5), ("a", 3), ("a", 1), ("r", 7), ("p", 7),
    ("a", 4), ("a", 6), ("a", 2), ("r", 3), ("p", 3), ("r", 1), ("p", 1),
    ("r", 4), ("p", 4), ("s", 2), ("r", 6), ("p", 6), ("s", 3),
    ("r", 2), ("p", 2), ("s", 1), ("r", 0), ("p", 0), ("s", 0),
)


def flip(index, bits):
    out = index
    bit = 1
    while bit <= bits:
        if bits & bit:
            out = out + bit - 2 * bit * (lax.div(index, bit) % 2)
        bit *= 2
    return out


def kernel(
    amp_ref, int_ref, out_ref, stage, held, slab, ysend, yrecv, zsum, zrecv,
    amp, whole, a2a_s, a2a_r, xf_s, xf_r, cf_s, cf_r, y_s, y_r, z_s, z_r, local_sem,
):
    cd = lax.axis_index("cd")
    ab = lax.axis_index("ab")
    rows, n_cd, width = amp_ref.shape
    wide = stage.shape[2]
    n_ab = slab.shape[0]
    columns = int_ref.shape[1]
    half = n_cd // 2

    load_amp = pltpu.make_async_copy(amp_ref, amp, local_sem.at[0])
    load_int = pltpu.make_async_copy(int_ref, whole, local_sem.at[1])
    load_amp.start()
    load_int.start()
    peers = [(flip(cd, k), ab) for k in range(1, n_cd)]
    peers += [(cd, flip(ab, 1)), (cd, flip(ab, 2))]
    peers += [(flip(cd, k), flip(ab, 2)) for k in DIRECT]
    barrier = pltpu.get_barrier_semaphore()
    for peer in peers:
        pl.semaphore_signal(barrier, inc=1, device_id=peer, device_id_type=MESH)

    stage[:, :, width:] = jnp.zeros((n_cd, rows, wide - width), stage.dtype)
    load_amp.wait()
    for c in range(n_cd):
        stage[c, :, :width] = amp[:, c, :]

    pl.semaphore_wait(barrier, len(peers))

    def remote(src, dst, s, r, peer):
        return pltpu.make_async_remote_copy(
            src_ref=src, dst_ref=dst, send_sem=s, recv_sem=r,
            device_id=peer, device_id_type=MESH,
        )

    def block(r, k):
        return held.at[r, k] if r or k else stage.at[cd]

    a2a, xf = {}, {}
    for k in ORDER:
        away = flip(cd, k)
        if k:
            a2a[k] = remote(stage.at[away], held.at[0, k], a2a_s.at[k], a2a_r.at[k], (away, ab))
            a2a[k].start()
        if k in DIRECT:
            xf[k] = remote(stage.at[away], held.at[2, k], xf_s.at[k], xf_r.at[k], (away, flip(ab, 2)))
            xf[k].start()
        else:
            xf[k] = remote(block(0, k), held.at[2, k], xf_s.at[k], xf_r.at[k], (cd, flip(ab, 2)))
    cf = {
        (r, k): remote(block(r, k), held.at[r + 1, k], cf_s.at[r // 2, k], cf_r.at[r // 2, k], (cd, flip(ab, 1)))
        for k in ORDER
        for r in (0, 2)
    }
    xf[0].start()
    cf[0, 0].start()

    load_int.wait()
    for j in range(n_ab):
        slab[j, :width, :] = whole[j * width : (j + 1) * width, :]
        slab[j, width:, :] = jnp.zeros((wide - width, columns), slab.dtype)

    ycopy = {
        h: remote(ysend.at[h], yrecv.at[h], y_s.at[h], y_r.at[h], (flip(cd, 1), ab)) for h in range(half)
    }
    zcopy = {
        h: remote(zsum.at[h], zrecv.at[h], z_s.at[h], z_r.at[h], (flip(cd, 2 * h), ab)) for h in range(1, half)
    }

    def arrive(k):
        a2a[k].wait_recv()
        if k not in DIRECT:
            xf[k].start()
        cf[0, k].start()

    def relay(k):
        xf[k].wait_recv()
        cf[2, k].start()

    def product(k):
        cf[0, k].wait_recv()
        cf[2, k].wait_recv()
        total = jnp.dot(block(0, k)[...], slab[ab], preferred_element_type=jnp.float32)
        for r in range(1, n_ab):
            total += jnp.dot(held[r, k], slab[flip(ab, r)], preferred_element_type=jnp.float32)
        if k % 2:
            ysend[k // 2] = total
            ycopy[k // 2].start()
        else:
            zsum[k // 2] = total

    def collect(h):
        ycopy[h].wait_recv()
        zsum[h] += yrecv[h]
        if h:
            zcopy[h].start()

    act = {"a": arrive, "r": relay, "p": product, "s": collect}
    for what, k in PLAN:
        act[what](k)
    total = zsum[0]
    for h in (2, 3, 1):
        zcopy[h].wait_recv()
        total += zrecv[h]
    out_ref[...] = total

    for k in ORDER:
        if k:
            a2a[k].wait_send()
        xf[k].wait_send()
        cf[0, k].wait_send()
        cf[2, k].wait_send()
    for h in range(half):
        ycopy[h].wait_send()
        if h:
            zcopy[h].wait_send()


def by_kernel(amplitudes, integrals, n_ab):
    rows, n_cd, width = amplitudes.shape
    columns = integrals.shape[2]
    wide = -(-width // LANES) * LANES
    half = n_cd // 2
    dma = pltpu.SemaphoreType.DMA
    block = pltpu.VMEM((half, rows, columns), jnp.float32)
    return pl.pallas_call(
        kernel,
        out_shape=jax.ShapeDtypeStruct((rows, columns), jnp.float32),
        in_specs=[pl.BlockSpec(memory_space=pltpu.HBM)] * 2,
        out_specs=pl.BlockSpec(memory_space=pltpu.VMEM),
        scratch_shapes=[
            pltpu.VMEM((n_cd, rows, wide), amplitudes.dtype),
            pltpu.VMEM((n_ab, n_cd, rows, wide), amplitudes.dtype),
            pltpu.VMEM((n_ab, wide, columns), integrals.dtype),
            block, block, block, block,
            pltpu.VMEM(amplitudes.shape, amplitudes.dtype),
            pltpu.VMEM(integrals.shape[1:], integrals.dtype),
            dma((n_cd,)), dma((n_cd,)), dma((n_cd,)), dma((n_cd,)),
            dma((2, n_cd)), dma((2, n_cd)),
            dma((half,)), dma((half,)), dma((half,)), dma((half,)),
            dma((2,)),
        ],
        compiler_params=pltpu.CompilerParams(
            collective_id=0, has_side_effects=True, vmem_limit_bytes=56 * 1024 * 1024
        ),
    )(amplitudes, integrals.reshape(integrals.shape[1], columns))


def by_collectives(amplitudes, integrals):
    c_local, depth, columns = integrals.shape
    mine = lax.all_to_all(amplitudes, "cd", split_axis=1, concat_axis=0, tiled=True)
    complete = lax.all_gather(mine, "ab", axis=2, tiled=True)
    flat = complete.reshape(complete.shape[0], c_local * depth)
    slab = integrals.reshape(c_local * depth, columns)
    partial = jnp.dot(flat, slab, preferred_element_type=jnp.float32)
    return lax.psum_scatter(partial, "cd", scatter_dimension=0, tiled=True)


def on_device(n_cd, n_ab, amplitudes, integrals):
    rows = amplitudes.shape[0]
    if n_cd == 8 and n_ab == 4 and integrals.shape[0] == 1 and rows % 16 == 0:
        return by_kernel(amplitudes, integrals, n_ab)
    return by_collectives(amplitudes, integrals)


def solution(mesh):
    specs = (P("cd", None, "ab"), P("cd", None, "ab"))
    return jax.shard_map(
        functools.partial(on_device, mesh.shape["cd"], mesh.shape["ab"]),
        mesh=mesh, in_specs=specs, out_specs=P("cd", "ab"), check_vma=False,
    )
```

profile of v0, /device:TPU:1, one launch (start us, length us, event | category | flops | bytes accessed | tf_op | source)
XLA Modules:
  0.0 35.1 jit_solution(1037223946229334081)
XLA Ops:
  0.0 33.5 %shard_map.28 = f32[64,512]{1,0:T(8,128)} custom-call(bf16[64,8,200]{2,1,0:T(8,128)(2,1)} %amp_ref.1, bf16[800,512]{1,0:T(8,128)(2,1)} %bitcast.1), custom_call_target="tpu_custom_call" | custom-call | tf_op jit(solution)/shard_map/pallas_call | solution.py:158
  33.5 1.6 %copy.4 = f32[64,512]{1,0:T(8,128)} copy(f32[64,512]{1,0:T(8,128)} %shard_map.28) | data formatting | bytes 262144
where the time goes:
time: 35.7 us; the launch traced here: 35.1 us
  Pallas kernels  33.5 us (94%)
  local copies, waits for them, and re-layouts  1.57 us (4%)
    pallas_call x1, Pallas kernels, by_kernel(): pl.pallas_call(kernel, out_shape=jax.ShapeDtypeStruct((rows, columns), jn...  33.5 us
    unnamed x1, local copies, waits for them, and re-layouts  1.57 us

commit v1 on v0

v1 whole, which is shorter than its diff:
```python
import functools

import jax
import jax.numpy as jnp
from jax import lax
from jax.experimental import pallas as pl
from jax.experimental.pallas import tpu as pltpu
from jax.sharding import PartitionSpec as P

MESH = pl.DeviceIdType.MESH
LANES = 128
FAR = (1, 3, 2)
PLAN = (
("a", 1), ("l", 0), ("r", 0), ("a", 3), ("a", 2), ("r", 1), ("p", 0), ("r", 3), ("r", 2), ("p", 1), ("y", 0), ("f", (1, 0)), ("p", 3), ("f", (3, 0)), ("p", 2), ("f", (2, 0)), ("f", (0, 0)),("y", 1), ("f", (3, 1)), ("f", (2, 1)), ("f", (1, 1)), ("f", (0, 1)), ("y", 2), ("f", (3, 2)), ("f", (2, 2)), ("f", (1, 2)), ("f", (0, 2)), ("y", 3), ("f", (3, 3)), ("f", (2, 3)), ("f", (1, 3)), ("f", (0, 3)),
)


def flip(index, bits):
    out = index
    bit = 1
    while bit <= bits:
        if bits & bit:
            out = out + bit - 2 * bit * (lax.div(index, bit) % 2)
        bit *= 2
    return out


def kernel(
    amp_ref, int_ref, part_ref, stage, held, slab, acc, amp, mine, other,
    sent, a_r, x_r, c_r, y_r, z_r, local_sem,
):
    cd = lax.axis_index("cd")
    ab = lax.axis_index("ab")
    rows, n_cd, width = amp_ref.shape
    wide = stage.shape[2]
    n_ab = slab.shape[1]
    n_z = held.shape[1]
    columns = int_ref.shape[1]
    pieces = columns // LANES
    both = (0, 1)

    load_amp = pltpu.make_async_copy(amp_ref, amp, local_sem.at[0])
    load_int = pltpu.make_async_copy(int_ref, mine, local_sem.at[1])
    load_amp.start()
    load_int.start()
    peers = [(flip(cd, k), ab) for k in (1, 2, 4, 6)]
    peers += [(cd, flip(ab, 1)), (cd, flip(ab, 2))]
    barrier = pltpu.get_barrier_semaphore()
    for peer in peers:
        pl.semaphore_signal(barrier, inc=1, device_id=peer, device_id_type=MESH)

    stage[:, :, width:] = jnp.zeros((n_cd, rows, wide - width), stage.dtype)
    load_amp.wait()
    for c in range(n_cd):
        stage[c, :, :width] = amp[:, c, :]
    for s in both:
        held[0, 0, s] = stage[flip(cd, s)]

    pl.semaphore_wait(barrier, len(peers))

    def remote(src, dst, s, r, peer):
        return pltpu.make_async_remote_copy(
            src_ref=src, dst_ref=dst, send_sem=s, recv_sem=r,
            device_id=peer, device_id_type=MESH,
        )

    def whole(like, sem):
        pltpu.make_async_copy(like, like, sem).wait()

    def cols(q):
        return pl.ds(q * LANES, LANES)

    acopy = {
        (k, s): remote(
            stage.at[flip(cd, 2 * k + s)], held.at[0, k, s], sent.at[0], a_r.at[k, s], (flip(cd, 2 * k), ab)
        )
        for k in FAR
        for s in both
    }
    xcopy = {
        (k, s): remote(held.at[0, k, s], held.at[2, k, s], sent.at[1], x_r.at[k, s], (cd, flip(ab, 2)))
        for k in range(n_z)
        for s in both
    }
    ccopy = {
        (r, k, s): remote(
            held.at[r, k, s], held.at[r + 1, k, s], sent.at[2], c_r.at[k], (cd, flip(ab, 1))
        )
        for r in (0, 2)
        for k in range(n_z)
        for s in both
    }
    ycopy = {
        q: remote(int_ref.at[:, cols(q)], other.at[:, cols(q)], sent.at[3], y_r.at[q], (flip(cd, 1), ab))
        for q in range(pieces)
    }
    zcopy = {
        (k, q): remote(acc.at[k, :, cols(q)], part_ref.at[k, :, cols(q)], sent.at[4], z_r.at[0], (flip(cd, 2 * k), ab))
        for k in FAR
        for q in range(pieces)
    }
    for s in both:
        xcopy[0, s].start()
        ccopy[0, 0, s].start()
    for k in FAR:
        for s in both:
            acopy[k, s].start()
    core = lax.rem(ab, 2)

    @pl.when(core == 0)
    def _():
        for q in range(pieces):
            ycopy[q].start()


    load_int.wait()
    for s in both:
        slab[s, :, width:, :] = jnp.zeros((n_ab, wide - width, columns), slab.dtype)
    for j in range(n_ab):
        slab[0, j, :width, :] = mine[j * width : (j + 1) * width, :]

    def arrive(k):
        for s in both:
            acopy[k, s].wait_recv()
            xcopy[k, s].start()
            ccopy[0, k, s].start()

    def relay(k):
        for s in both:
            xcopy[k, s].wait_recv()
            ccopy[2, k, s].start()

    def product(k):
        whole(held.at[0:2, k], c_r.at[k])
        total = jnp.dot(held[0, k, 0], slab[0, ab], preferred_element_type=jnp.float32)
        for r in range(1, n_ab):
            total += jnp.dot(held[r, k, 0], slab[0, flip(ab, r)], preferred_element_type=jnp.float32)
        acc[k] = total

    def piece(q):
        ycopy[q].wait_recv()
        here = slice(q * LANES, (q + 1) * LANES)
        for j in range(n_ab):
            slab[1, j, :width, here] = other[j * width : (j + 1) * width, here]

    def finish(kq):
        k, q = kq
        here = slice(q * LANES, (q + 1) * LANES)
        total = acc[k, :, here]
        for r in range(n_ab):
            total += jnp.dot(held[r, k, 1], slab[1, flip(ab, r), :, here], preferred_element_type=jnp.float32)
        acc[k, :, here] = total
        if k:
            zcopy[k, q].start()

    def late(k):
        @pl.when(core == 1)
        def _():
            for q in range(pieces):
                ycopy[q].start()

    act = {"l": late, "a": arrive, "r": relay, "p": product, "y": piece, "f": finish}
    for what, k in PLAN:
        act[what](k)
    own = pltpu.make_async_copy(acc.at[0], part_ref.at[0], local_sem.at[2])
    own.start()
    own.wait()
    whole(held.at[0, 1:], sent.at[0])
    whole(held.at[0], sent.at[1])
    whole(held.at[0:2], sent.at[2])
    whole(other, sent.at[3])
    whole(acc.at[1:], sent.at[4])
    whole(acc.at[1:], z_r.at[0])


def by_kernel(amplitudes, integrals, n_ab):
    rows, n_cd, width = amplitudes.shape
    columns = integrals.shape[2]
    wide = -(-width // LANES) * LANES
    n_z = n_cd // 2
    pieces = columns // LANES
    dma = pltpu.SemaphoreType.DMA
    parts = pl.pallas_call(
        kernel,
        out_shape=jax.ShapeDtypeStruct((n_z, rows, columns), jnp.float32),
        in_specs=[pl.BlockSpec(memory_space=pltpu.HBM)] * 2,
        out_specs=pl.BlockSpec(memory_space=pltpu.HBM),
        scratch_shapes=[
            pltpu.VMEM((n_cd, rows, wide), amplitudes.dtype),
            pltpu.VMEM((n_ab, n_z, 2, rows, wide), amplitudes.dtype),
            pltpu.VMEM((2, n_ab, wide, columns), integrals.dtype),
            pltpu.VMEM((n_z, rows, columns), jnp.float32),
            pltpu.VMEM(amplitudes.shape, amplitudes.dtype),
            pltpu.VMEM(integrals.shape[1:], integrals.dtype),
            pltpu.VMEM(integrals.shape[1:], integrals.dtype),
            dma((5,)), dma((n_z, 2)), dma((n_z, 2)), dma((n_z,)), dma((pieces,)), dma((1,)),
            dma((3,)),
        ],
        compiler_params=pltpu.CompilerParams(
            collective_id=0, has_side_effects=True, vmem_limit_bytes=56 * 1024 * 1024
        ),
    )(amplitudes, integrals.reshape(integrals.shape[1], columns))
    return jnp.sum(parts, axis=0)


def by_collectives(amplitudes, integrals):
    c_local, depth, columns = integrals.shape
    mine = lax.all_to_all(amplitudes, "cd", split_axis=1, concat_axis=0, tiled=True)
    complete = lax.all_gather(mine, "ab", axis=2, tiled=True)
    flat = complete.reshape(complete.shape[0], c_local * depth)
    slab = integrals.reshape(c_local * depth, columns)
    partial = jnp.dot(flat, slab, preferred_element_type=jnp.float32)
    return lax.psum_scatter(partial, "cd", scatter_dimension=0, tiled=True)


def on_device(n_cd, n_ab, amplitudes, integrals):
    rows = amplitudes.shape[0]
    columns = integrals.shape[2]
    if n_cd == 8 and n_ab == 4 and integrals.shape[0] == 1 and rows % 16 == 0 and columns % LANES == 0:
        return by_kernel(amplitudes, integrals, n_ab)
    return by_collectives(amplitudes, integrals)


def solution(mesh):
    specs = (P("cd", None, "ab"), P("cd", None, "ab"))
    return jax.shard_map(
        functools.partial(on_device, mesh.shape["cd"], mesh.shape["ab"]),
        mesh=mesh, in_specs=specs, out_specs=P("cd", "ab"), check_vma=False,
    )
```

time: 35.7 us -> 31.4 us (0.88)
  Pallas kernels: 33.5 us -> 29.1 us
  other arithmetic: 0 us -> 1.74 us
  local copies, waits for them, and re-layouts: 1.57 us -> 0 us
    pallas_call x1, Pallas kernels: 33.5 us -> 29.1 us  [by_kernel(): pl.pallas_call(kernel, out_shape=jax.ShapeDtypeStruct((n_z, rows, columns...]
    reduce_sum x0 -> x1, other arithmetic: none -> 1.74 us  [by_kernel(): return jnp.sum(parts, axis=0)]
    unnamed x1 -> x0, local copies, waits for them, and re-layouts: 1.57 us -> none
where the time goes in v1:
time: 31.4 us; the launch traced here: 30.9 us
  Pallas kernels  29.1 us (93%)
  other arithmetic  1.74 us (6%)
    pallas_call x1, Pallas kernels, by_kernel(): pl.pallas_call(kernel, out_shape=jax.ShapeDtypeStruct((n_z, rows, columns...  29.1 us
    reduce_sum x1, other arithmetic, by_kernel(): return jnp.sum(parts, axis=0)  1.74 us

profile of v1, /device:TPU:1, one launch (start us, length us, event | category | flops | bytes accessed | tf_op | source)
XLA Modules:
  0.0 30.9 jit_solution(1375600407025349538)
XLA Ops:
  0.0 29.1 %shard_map.28 = f32[4,64,512]{2,1,0:T(8,128)} custom-call(bf16[64,8,200]{2,1,0:T(8,128)(2,1)} %amp_ref.1, bf16[800,512]{1,0:T(8,128)(2,1)} %bitcast.1), custom_call_target="tpu_custom_call" | custom-call | tf_op jit(solution)/shard_map/pallas_call | solution.py:183
  29.1 1.7 %reduce_sum.9 = f32[64,512]{1,0:T(8,128)} reduce(f32[4,64,512]{2,1,0:T(8,128)} %shard_map.28, f32[]{:T(128)} %constant.0.clone.1), dimensions={0}, to_apply=%region_0.0 | reduce | flops 98304 | bytes 655364 | tf_op jit(solution)/shard_map/reduce_sum | solution.py:203

commit v2 on v1

--- a/solution.py
+++ b/solution.py
@@ -67,6 +67,9 @@
     def whole(like, sem):
         pltpu.make_async_copy(like, like, sem).wait()
 
+    def sums(k):
+        return acc.at[k] if k else part_ref.at[0]
+
     def cols(q):
         return pl.ds(q * LANES, LANES)
 
@@ -91,7 +94,7 @@
         for s in both
     }
     ycopy = {
-        q: remote(int_ref.at[:, cols(q)], other.at[:, cols(q)], sent.at[3], y_r.at[q], (flip(cd, 1), ab))
+        q: remote(mine.at[:, cols(q)], other.at[:, cols(q)], sent.at[3], y_r.at[q], (flip(cd, 1), ab))
         for q in range(pieces)
     }
     zcopy = {
@@ -107,13 +110,14 @@
             acopy[k, s].start()
     core = lax.rem(ab, 2)
 
+    load_int.wait()
+
     @pl.when(core == 0)
     def _():
         for q in range(pieces):
             ycopy[q].start()
 
 
-    load_int.wait()
     for s in both:
         slab[s, :, width:, :] = jnp.zeros((n_ab, wide - width, columns), slab.dtype)
     for j in range(n_ab):
@@ -135,7 +139,7 @@
         total = jnp.dot(held[0, k, 0], slab[0, ab], preferred_element_type=jnp.float32)
         for r in range(1, n_ab):
             total += jnp.dot(held[r, k, 0], slab[0, flip(ab, r)], preferred_element_type=jnp.float32)
-        acc[k] = total
+        sums(k)[...] = total
 
     def piece(q):
         ycopy[q].wait_recv()
@@ -146,10 +150,10 @@
     def finish(kq):
         k, q = kq
         here = slice(q * LANES, (q + 1) * LANES)
-        total = acc[k, :, here]
+        total = sums(k)[:, here]
         for r in range(n_ab):
             total += jnp.dot(held[r, k, 1], slab[1, flip(ab, r), :, here], preferred_element_type=jnp.float32)
-        acc[k, :, here] = total
+        sums(k)[:, here] = total
         if k:
             zcopy[k, q].start()
 
@@ -162,9 +166,6 @@
     act = {"l": late, "a": arrive, "r": relay, "p": product, "y": piece, "f": finish}
     for what, k in PLAN:
         act[what](k)
-    own = pltpu.make_async_copy(acc.at[0], part_ref.at[0], local_sem.at[2])
-    own.start()
-    own.wait()
     whole(held.at[0, 1:], sent.at[0])
     whole(held.at[0], sent.at[1])
     whole(held.at[0:2], sent.at[2])
@@ -182,9 +183,9 @@
     dma = pltpu.SemaphoreType.DMA
     parts = pl.pallas_call(
         kernel,
-        out_shape=jax.ShapeDtypeStruct((n_z, rows, columns), jnp.float32),
+        out_shape=pltpu.VMEM((n_z, rows, columns), jnp.float32),
         in_specs=[pl.BlockSpec(memory_space=pltpu.HBM)] * 2,
-        out_specs=pl.BlockSpec(memory_space=pltpu.HBM),
+        out_specs=pl.BlockSpec(memory_space=pltpu.VMEM),
         scratch_shapes=[
             pltpu.VMEM((n_cd, rows, wide), amplitudes.dtype),
             pltpu.VMEM((n_ab, n_z, 2, rows, wide), amplitudes.dtype),
@@ -194,12 +195,15 @@
             pltpu.VMEM(integrals.shape[1:], integrals.dtype),
             pltpu.VMEM(integrals.shape[1:], integrals.dtype),
             dma((5,)), dma((n_z, 2)), dma((n_z, 2)), dma((n_z,)), dma((pieces,)), dma((1,)),
-            dma((3,)),
+            dma((2,)),
         ],
         compiler_params=pltpu.CompilerParams(
-            collective_id=0, has_side_effects=True, vmem_limit_bytes=56 * 1024 * 1024
+            collective_id=0, has_side_effects=True, vmem_limit_bytes=32 * 1024 * 1024
         ),
-    )(amplitudes, integrals.reshape(integrals.shape[1], columns))
+    )(
+        pltpu.with_memory_space_constraint(amplitudes, pltpu.HBM),
+        pltpu.with_memory_space_constraint(integrals.reshape(integrals.shape[1], columns), pltpu.HBM),
+    )
     return jnp.sum(parts, axis=0)
 
 

time: 31.4 us -> 30 us (0.955)
  other arithmetic: 1.74 us -> 0.69 us
    reduce_sum x1, other arithmetic: 1.74 us -> 0.69 us  [by_kernel(): return jnp.sum(parts, axis=0)]
    pallas_call x1, Pallas kernels: 29.1 us -> 28.8 us  [by_kernel(): pl.pallas_call(kernel, out_shape=pltpu.VMEM((n_z, rows, columns), jnp.flo...]
where the time goes in v2:
time: 30 us; the launch traced here: 29.5 us
  Pallas kernels  28.8 us (96%)
  other arithmetic  0.69 us (2%)
    pallas_call x1, Pallas kernels, by_kernel(): pl.pallas_call(kernel, out_shape=pltpu.VMEM((n_z, rows, columns), jnp.flo...  28.8 us
    reduce_sum x1, other arithmetic, by_kernel(): return jnp.sum(parts, axis=0)  0.69 us

profile of v2, /device:TPU:1, one launch (start us, length us, event | category | flops | bytes accessed | tf_op | source)
XLA Modules:
  0.0 29.5 jit_solution(2385162442266687469)
XLA Ops:
  0.0 28.8 %shard_map.28 = f32[4,64,512]{2,1,0:T(8,128)S(1)} custom-call(bf16[64,8,200]{2,1,0:T(8,128)(2,1)} %amp_ref.1, bf16[800,512]{1,0:T(8,128)(2,1)} %bitcast.1), custom_call_target="tpu_custom_call" | custom-call | tf_op jit(solution)/shard_map/pallas_call | solution.py:184
  28.8 0.7 %reduce_sum.9 = f32[64,512]{1,0:T(8,128)} reduce(f32[4,64,512]{2,1,0:T(8,128)S(1)} %shard_map.28, f32[]{:T(128)} %constant.0.clone.1), dimensions={0}, to_apply=%region_0.0 | reduce | flops 98304 | bytes 655364 | tf_op jit(solution)/shard_map/reduce_sum | solution.py:207

commit v3 on v2

--- a/solution.py
+++ b/solution.py
@@ -9,9 +9,10 @@
 
 MESH = pl.DeviceIdType.MESH
 LANES = 128
+VIA = 1
 FAR = (1, 3, 2)
 PLAN = (
-("a", 1), ("l", 0), ("r", 0), ("a", 3), ("a", 2), ("r", 1), ("p", 0), ("r", 3), ("r", 2), ("p", 1), ("y", 0), ("f", (1, 0)), ("p", 3), ("f", (3, 0)), ("p", 2), ("f", (2, 0)), ("f", (0, 0)),("y", 1), ("f", (3, 1)), ("f", (2, 1)), ("f", (1, 1)), ("f", (0, 1)), ("y", 2), ("f", (3, 2)), ("f", (2, 2)), ("f", (1, 2)), ("f", (0, 2)), ("y", 3), ("f", (3, 3)), ("f", (2, 3)), ("f", (1, 3)), ("f", (0, 3)),
+    ("a", 1), ("a", 3), ("r", 0), ("r", 1), ("a", 2), ("p", 1), ("y", 0), ("f", (1, 0)), ("r", 3), ("p", 0), ("r", 2), ("p", 3), ("f", (3, 0)), ("p", 2), ("f", (2, 0)), ("y", 1), ("f", (3, 1)), ("f", (2, 1)), ("f", (1, 1)), ("f", (0, 0)), ("f", (0, 1)), ("h", 0), ("y", 2), ("f", (3, 2)), ("f", (2, 2)), ("f", (1, 2)), ("f", (0, 2)), ("y", 3), ("f", (3, 3)), ("f", (2, 3)), ("f", (1, 3)), ("f", (0, 3)),
 )
 
 
@@ -26,8 +27,8 @@
 
 
 def kernel(
-    amp_ref, int_ref, part_ref, stage, held, slab, acc, amp, mine, other,
-    sent, a_r, x_r, c_r, y_r, z_r, local_sem,
+    amp_ref, int_ref, part_ref, stage, held, slab, acc, amp, mine, other, lent,
+    sent, a_r, x_r, c_r, y_r, l_r, z_r, h_r, near, local_sem,
 ):
     cd = lax.axis_index("cd")
     ab = lax.axis_index("ab")
@@ -40,11 +41,15 @@
     both = (0, 1)
 
     load_amp = pltpu.make_async_copy(amp_ref, amp, local_sem.at[0])
-    load_int = pltpu.make_async_copy(int_ref, mine, local_sem.at[1])
+    load_int = [
+        pltpu.make_async_copy(int_ref.at[:, pl.ds(q * LANES, LANES)], mine.at[q], local_sem.at[1])
+        for q in range(pieces)
+    ]
     load_amp.start()
-    load_int.start()
+    for q in range(pieces):
+        load_int[q].start()
     peers = [(flip(cd, k), ab) for k in (1, 2, 4, 6)]
-    peers += [(cd, flip(ab, 1)), (cd, flip(ab, 2))]
+    peers += [(cd, flip(ab, 1)), (cd, flip(ab, 2)), (flip(cd, 1), flip(ab, 1))]
     barrier = pltpu.get_barrier_semaphore()
     for peer in peers:
         pl.semaphore_signal(barrier, inc=1, device_id=peer, device_id_type=MESH)
@@ -93,14 +98,29 @@
         for k in range(n_z)
         for s in both
     }
+    deep = lent.shape[1]
+    lend = {
+        q: remote(mine.at[q, deep:], lent.at[q], sent.at[7], l_r.at[q], (cd, flip(ab, 1)))
+        for q in range(pieces)
+    }
     ycopy = {
-        q: remote(mine.at[:, cols(q)], other.at[:, cols(q)], sent.at[3], y_r.at[q], (flip(cd, 1), ab))
+        q: remote(mine.at[q, :deep], other.at[q, :deep], sent.at[3], y_r.at[q], (flip(cd, 1), ab))
+        for q in range(pieces)
+    }
+    lcopy = {
+        q: remote(lent.at[q], other.at[q, deep:], sent.at[3], y_r.at[q], (flip(cd, 1), flip(ab, 1)))
         for q in range(pieces)
     }
     zcopy = {
-        (k, q): remote(acc.at[k, :, cols(q)], part_ref.at[k, :, cols(q)], sent.at[4], z_r.at[0], (flip(cd, 2 * k), ab))
+        (k, q): remote(
+            acc.at[k, :, cols(q)], part_ref.at[k, :, cols(q)], sent.at[3 + k], z_r.at[k], (flip(cd, 2 * k), ab)
+        )
         for k in FAR
         for q in range(pieces)
+        if k < 3 or q >= VIA
+    }
+    hcopy = {
+        q: remote(acc.at[3, :, cols(q)], near.at[q], sent.at[8], h_r.at[q], (flip(cd, 2), ab)) for q in range(VIA)
     }
     for s in both:
         xcopy[0, s].start()
@@ -109,19 +129,32 @@
         for s in both:
             acopy[k, s].start()
     core = lax.rem(ab, 2)
-
-    load_int.wait()
+    whole(mine, local_sem.at[1])
+    ycopy[0].start()
+    for q in range(pieces):
+        lend[q].start()
 
     @pl.when(core == 0)
     def _():
         for q in range(pieces):
-            ycopy[q].start()
-
+            if q:
+                ycopy[q].start()
+            lend[q].wait_recv()
+            lcopy[q].start()
+
+    @pl.when(core == 1)
+    def _():
+        for q in range(pieces):
+            lend[q].wait_recv()
+            lcopy[q].start()
+            if q:
+                ycopy[q].start()
 
     for s in both:
         slab[s, :, width:, :] = jnp.zeros((n_ab, wide - width, columns), slab.dtype)
     for j in range(n_ab):
-        slab[0, j, :width, :] = mine[j * width : (j + 1) * width, :]
+        for q in range(pieces):
+            slab[0, j, :width, q * LANES : (q + 1) * LANES] = mine[q, j * width : (j + 1) * width, :]
 
     def arrive(k):
         for s in both:
@@ -142,10 +175,10 @@
         sums(k)[...] = total
 
     def piece(q):
-        ycopy[q].wait_recv()
+        whole(other.at[q], y_r.at[q])
         here = slice(q * LANES, (q + 1) * LANES)
         for j in range(n_ab):
-            slab[1, j, :width, here] = other[j * width : (j + 1) * width, here]
+            slab[1, j, :width, here] = other[q, j * width : (j + 1) * width, :]
 
     def finish(kq):
         k, q = kq
@@ -154,24 +187,31 @@
         for r in range(n_ab):
             total += jnp.dot(held[r, k, 1], slab[1, flip(ab, r), :, here], preferred_element_type=jnp.float32)
         sums(k)[:, here] = total
-        if k:
+        if k == 3 and q < VIA:
+            hcopy[q].start()
+        elif k == 1 or k and q >= VIA:
             zcopy[k, q].start()
 
-    def late(k):
-        @pl.when(core == 1)
-        def _():
-            for q in range(pieces):
-                ycopy[q].start()
-
-    act = {"l": late, "a": arrive, "r": relay, "p": product, "y": piece, "f": finish}
+    def pass_on(q):
+        h = slice(q * LANES, (q + 1) * LANES)
+        hcopy[q].wait_recv()
+        acc[2, :, h] += near[q]
+        zcopy[2, q].start()
+
+    part_ref[3, :, : VIA * LANES] = jnp.zeros((rows, VIA * LANES), part_ref.dtype)
+    act = {"a": arrive, "r": relay, "p": product, "y": piece, "f": finish, "h": pass_on}
     for what, k in PLAN:
         act[what](k)
     whole(held.at[0, 1:], sent.at[0])
+    whole(near, sent.at[8])
     whole(held.at[0], sent.at[1])
     whole(held.at[0:2], sent.at[2])
     whole(other, sent.at[3])
-    whole(acc.at[1:], sent.at[4])
-    whole(acc.at[1:], z_r.at[0])
+    whole(lent, sent.at[7])
+    for k in FAR:
+        direct = acc.at[k, :, VIA * LANES :] if k == 3 else acc.at[k]
+        whole(direct, sent.at[3 + k])
+        whole(direct, z_r.at[k])
 
 
 def by_kernel(amplitudes, integrals, n_ab):
@@ -192,9 +232,10 @@
             pltpu.VMEM((2, n_ab, wide, columns), integrals.dtype),
             pltpu.VMEM((n_z, rows, columns), jnp.float32),
             pltpu.VMEM(amplitudes.shape, amplitudes.dtype),
-            pltpu.VMEM(integrals.shape[1:], integrals.dtype),
-            pltpu.VMEM(integrals.shape[1:], integrals.dtype),
-            dma((5,)), dma((n_z, 2)), dma((n_z, 2)), dma((n_z,)), dma((pieces,)), dma((1,)),
+            pltpu.VMEM((pieces, integrals.shape[1], LANES), integrals.dtype),
+            pltpu.VMEM((pieces, integrals.shape[1], LANES), integrals.dtype),
+            pltpu.VMEM((pieces, integrals.shape[1] // 2, LANES), integrals.dtype),
+            dma((9,)), dma((n_z, 2)), dma((n_z, 2)), dma((n_z,)), dma((pieces,)), dma((pieces,)), dma((n_z,)), dma((VIA,)), pltpu.VMEM((VIA, rows, LANES), jnp.float32),
             dma((2,)),
         ],
         compiler_params=pltpu.CompilerParams(
@@ -220,7 +261,7 @@
 def on_device(n_cd, n_ab, amplitudes, integrals):
     rows = amplitudes.shape[0]
     columns = integrals.shape[2]
-    if n_cd == 8 and n_ab == 4 and integrals.shape[0] == 1 and rows % 16 == 0 and columns % LANES == 0:
+    if n_cd == 8 and n_ab == 4 and integrals.shape[0] == 1 and rows % 16 == 0 and columns % LANES == 0 and integrals.shape[1] % 32 == 0:
         return by_kernel(amplitudes, integrals, n_ab)
     return by_collectives(amplitudes, integrals)
 

time: 30 us -> 29.3 us (0.977)
  Pallas kernels: 28.8 us -> 28.3 us
    pallas_call x1, Pallas kernels: 28.8 us -> 28.3 us  [by_kernel(): pl.pallas_call(kernel, out_shape=pltpu.VMEM((n_z, rows, columns), jnp.flo...]
where the time goes in v3:
time: 29.3 us; the launch traced here: 29 us
  Pallas kernels  28.3 us (97%)
  other arithmetic  0.69 us (2%)
    pallas_call x1, Pallas kernels, by_kernel(): pl.pallas_call(kernel, out_shape=pltpu.VMEM((n_z, rows, columns), jnp.flo...  28.3 us
    reduce_sum x1, other arithmetic, by_kernel(): return jnp.sum(parts, axis=0)  0.69 us

profile of v3, /device:TPU:1, one launch (start us, length us, event | category | flops | bytes accessed | tf_op | source)
XLA Modules:
  0.0 29.0 jit_solution(15361347783182737419)
XLA Ops:
  0.0 28.3 %shard_map.28 = f32[4,64,512]{2,1,0:T(8,128)S(1)} custom-call(bf16[64,8,200]{2,1,0:T(8,128)(2,1)} %amp_ref.1, bf16[800,512]{1,0:T(8,128)(2,1)} %bitcast.1), custom_call_target="tpu_custom_call" | custom-call | tf_op jit(solution)/shard_map/pallas_call | solution.py:224
  28.3 0.7 %reduce_sum.9 = f32[64,512]{1,0:T(8,128)} reduce(f32[4,64,512]{2,1,0:T(8,128)S(1)} %shard_map.28, f32[]{:T(128)} %constant.0.clone.1), dimensions={0}, to_apply=%region_0.0 | reduce | flops 98304 | bytes 655364 | tf_op jit(solution)/shard_map/reduce_sum | solution.py:248

commit v4 on v3

--- a/solution.py
+++ b/solution.py
@@ -12,7 +12,7 @@
 VIA = 1
 FAR = (1, 3, 2)
 PLAN = (
-    ("a", 1), ("a", 3), ("r", 0), ("r", 1), ("a", 2), ("p", 1), ("y", 0), ("f", (1, 0)), ("r", 3), ("p", 0), ("r", 2), ("p", 3), ("f", (3, 0)), ("p", 2), ("f", (2, 0)), ("y", 1), ("f", (3, 1)), ("f", (2, 1)), ("f", (1, 1)), ("f", (0, 0)), ("f", (0, 1)), ("h", 0), ("y", 2), ("f", (3, 2)), ("f", (2, 2)), ("f", (1, 2)), ("f", (0, 2)), ("y", 3), ("f", (3, 3)), ("f", (2, 3)), ("f", (1, 3)), ("f", (0, 3)),
+    ("a", 1), ("a", 3), ("r", 0), ("r", 1), ("a", 2), ("p", 1), ("y", 0), ("f", (1, 0)), ("r", 3), ("p", 0), ("r", 2), ("p", 3), ("f", (3, 0)), ("p", 2), ("f", (2, 0)), ("y", 1), ("f", (3, 1)), ("f", (2, 1)), ("f", (1, 1)), ("f", (0, 0)), ("f", (0, 1)), ("i", 0), ("y", 2), ("f", (3, 2)), ("f", (2, 2)), ("f", (1, 2)), ("f", (0, 2)), ("j", 0), ("y", 3), ("f", (3, 3)), ("f", (2, 3)), ("f", (1, 3)), ("f", (0, 3)),
 )
 
 
@@ -198,8 +198,18 @@
         acc[2, :, h] += near[q]
         zcopy[2, q].start()
 
+    def pass_first(q):
+        @pl.when(core == 1)
+        def _():
+            pass_on(q)
+
+    def pass_later(q):
+        @pl.when(core == 0)
+        def _():
+            pass_on(q)
+
     part_ref[3, :, : VIA * LANES] = jnp.zeros((rows, VIA * LANES), part_ref.dtype)
-    act = {"a": arrive, "r": relay, "p": product, "y": piece, "f": finish, "h": pass_on}
+    act = {"a": arrive, "r": relay, "p": product, "y": piece, "f": finish, "h": pass_on, "i": pass_first, "j": pass_later}
     for what, k in PLAN:
         act[what](k)
     whole(held.at[0, 1:], sent.at[0])

time: 29.3 us -> 29.1 us (level)
  no operation moved by 1% of the time
where the time goes in v4:
time: 29.1 us; the launch traced here: 29 us
  Pallas kernels  28.3 us (97%)
  other arithmetic  0.69 us (2%)
    pallas_call x1, Pallas kernels, by_kernel(): pl.pallas_call(kernel, out_shape=pltpu.VMEM((n_z, rows, columns), jnp.flo...  28.3 us
    reduce_sum x1, other arithmetic, by_kernel(): return jnp.sum(parts, axis=0)  0.69 us

profile of v4, /device:TPU:1, one launch (start us, length us, event | category | flops | bytes accessed | tf_op | source)
XLA Modules:
  0.0 29.0 jit_solution(5772561843741216613)
XLA Ops:
  0.0 28.3 %shard_map.28 = f32[4,64,512]{2,1,0:T(8,128)S(1)} custom-call(bf16[64,8,200]{2,1,0:T(8,128)(2,1)} %amp_ref.1, bf16[800,512]{1,0:T(8,128)(2,1)} %bitcast.1), custom_call_target="tpu_custom_call" | custom-call | tf_op jit(solution)/shard_map/pallas_call | solution.py:234
  28.3 0.7 %reduce_sum.9 = f32[64,512]{1,0:T(8,128)} reduce(f32[4,64,512]{2,1,0:T(8,128)S(1)} %shard_map.28, f32[]{:T(128)} %constant.0.clone.1), dimensions={0}, to_apply=%region_0.0 | reduce | flops 98304 | bytes 655364 | tf_op jit(solution)/shard_map/reduce_sum | solution.py:258

commit v5 on v4

--- a/solution.py
+++ b/solution.py
@@ -12,7 +12,7 @@
 VIA = 1
 FAR = (1, 3, 2)
 PLAN = (
-    ("a", 1), ("a", 3), ("r", 0), ("r", 1), ("a", 2), ("p", 1), ("y", 0), ("f", (1, 0)), ("r", 3), ("p", 0), ("r", 2), ("p", 3), ("f", (3, 0)), ("p", 2), ("f", (2, 0)), ("y", 1), ("f", (3, 1)), ("f", (2, 1)), ("f", (1, 1)), ("f", (0, 0)), ("f", (0, 1)), ("i", 0), ("y", 2), ("f", (3, 2)), ("f", (2, 2)), ("f", (1, 2)), ("f", (0, 2)), ("j", 0), ("y", 3), ("f", (3, 3)), ("f", (2, 3)), ("f", (1, 3)), ("f", (0, 3)),
+    ("a", 1), ("a", 3), ("r", 0), ("r", 1), ("a", 2), ("p", 1), ("y", 0), ("f", (1, 0)), ("r", 3), ("p", 0), ("r", 2), ("p", 3), ("f", (3, 0)), ("p", 2), ("f", (2, 0)), ("y", 1), ("f", (3, 1)), ("f", (2, 1)), ("f", (1, 1)), ("f", (0, 0)), ("f", (0, 1)), ("i", 0), ("y", 2), ("f", (3, 2)), ("f", (2, 2)), ("f", (1, 2)), ("f", (0, 2)), ("j", 0), ("y", 3), ("f", (2, 3)), ("f", (3, 3)), ("f", (1, 3)), ("f", (0, 3)),
 )
 
 
@@ -27,7 +27,7 @@
 
 
 def kernel(
-    amp_ref, int_ref, part_ref, stage, held, slab, acc, amp, mine, other, lent,
+    amp_ref, int_ref, out_ref, part_ref, stage, held, slab, acc, amp, mine, other, lent,
     sent, a_r, x_r, c_r, y_r, l_r, z_r, h_r, near, local_sem,
 ):
     cd = lax.axis_index("cd")
@@ -80,7 +80,7 @@
 
     acopy = {
         (k, s): remote(
-            stage.at[flip(cd, 2 * k + s)], held.at[0, k, s], sent.at[0], a_r.at[k, s], (flip(cd, 2 * k), ab)
+            stage.at[flip(cd, 2 * k + s)], held.at[0, k, s], sent.at[0], a_r.at[k - 1, s], (flip(cd, 2 * k), ab)
         )
         for k in FAR
         for s in both
@@ -100,7 +100,7 @@
     }
     deep = lent.shape[1]
     lend = {
-        q: remote(mine.at[q, deep:], lent.at[q], sent.at[7], l_r.at[q], (cd, flip(ab, 1)))
+        q: remote(mine.at[q, deep:], lent.at[q], sent.at[5], l_r.at[q], (cd, flip(ab, 1)))
         for q in range(pieces)
     }
     ycopy = {
@@ -113,14 +113,14 @@
     }
     zcopy = {
         (k, q): remote(
-            acc.at[k, :, cols(q)], part_ref.at[k, :, cols(q)], sent.at[3 + k], z_r.at[k], (flip(cd, 2 * k), ab)
+            acc.at[k, :, cols(q)], part_ref.at[k, :, cols(q)], sent.at[4], z_r.at[k - 1, q // (pieces - 1)], (flip(cd, 2 * k), ab)
         )
         for k in FAR
         for q in range(pieces)
         if k < 3 or q >= VIA
     }
     hcopy = {
-        q: remote(acc.at[3, :, cols(q)], near.at[q], sent.at[8], h_r.at[q], (flip(cd, 2), ab)) for q in range(VIA)
+        q: remote(acc.at[3, :, cols(q)], near.at[q], sent.at[4], h_r.at[q], (flip(cd, 2), ab)) for q in range(VIA)
     }
     for s in both:
         xcopy[0, s].start()
@@ -213,15 +213,18 @@
     for what, k in PLAN:
         act[what](k)
     whole(held.at[0, 1:], sent.at[0])
-    whole(near, sent.at[8])
     whole(held.at[0], sent.at[1])
     whole(held.at[0:2], sent.at[2])
     whole(other, sent.at[3])
-    whole(lent, sent.at[7])
-    for k in FAR:
-        direct = acc.at[k, :, VIA * LANES :] if k == 3 else acc.at[k]
-        whole(direct, sent.at[3 + k])
-        whole(direct, z_r.at[k])
+    whole(lent, sent.at[5])
+    whole(acc.at[1:], sent.at[4])
+    early = (pieces - 1) * LANES
+    for first, last, n in ((0, early, 0), (early, columns, 1)):
+        for k in FAR:
+            begin = VIA * LANES if k == 3 and not n else first
+            whole(acc.at[k, :, begin:last], z_r.at[k - 1, n])
+        h = slice(first, last)
+        out_ref[:, h] = (part_ref[0, :, h] + part_ref[1, :, h]) + (part_ref[2, :, h] + part_ref[3, :, h])
 
 
 def by_kernel(amplitudes, integrals, n_ab):
@@ -231,12 +234,13 @@
     n_z = n_cd // 2
     pieces = columns // LANES
     dma = pltpu.SemaphoreType.DMA
-    parts = pl.pallas_call(
+    return pl.pallas_call(
         kernel,
-        out_shape=pltpu.VMEM((n_z, rows, columns), jnp.float32),
+        out_shape=pltpu.VMEM((rows, columns), jnp.float32),
         in_specs=[pl.BlockSpec(memory_space=pltpu.HBM)] * 2,
         out_specs=pl.BlockSpec(memory_space=pltpu.VMEM),
         scratch_shapes=[
+            pltpu.VMEM((n_z, rows, columns), jnp.float32),
             pltpu.VMEM((n_cd, rows, wide), amplitudes.dtype),
             pltpu.VMEM((n_ab, n_z, 2, rows, wide), amplitudes.dtype),
             pltpu.VMEM((2, n_ab, wide, columns), integrals.dtype),
@@ -245,7 +249,7 @@
             pltpu.VMEM((pieces, integrals.shape[1], LANES), integrals.dtype),
             pltpu.VMEM((pieces, integrals.shape[1], LANES), integrals.dtype),
             pltpu.VMEM((pieces, integrals.shape[1] // 2, LANES), integrals.dtype),
-            dma((9,)), dma((n_z, 2)), dma((n_z, 2)), dma((n_z,)), dma((pieces,)), dma((pieces,)), dma((n_z,)), dma((VIA,)), pltpu.VMEM((VIA, rows, LANES), jnp.float32),
+            dma((6,)), dma((n_z - 1, 2)), dma((n_z, 2)), dma((n_z,)), dma((pieces,)), dma((pieces,)), dma((n_z - 1, 2)), dma((VIA,)), pltpu.VMEM((VIA, rows, LANES), jnp.float32),
             dma((2,)),
         ],
         compiler_params=pltpu.CompilerParams(
@@ -255,7 +259,6 @@
         pltpu.with_memory_space_constraint(amplitudes, pltpu.HBM),
         pltpu.with_memory_space_constraint(integrals.reshape(integrals.shape[1], columns), pltpu.HBM),
     )
-    return jnp.sum(parts, axis=0)
 
 
 def by_collectives(amplitudes, integrals):

time: 29.1 us -> 28.7 us (0.986)
  other arithmetic: 0.69 us -> 0 us
  local copies, waits for them, and re-layouts: 0 us -> 0.66 us
  Pallas kernels: 28.3 us -> 27.9 us
    reduce_sum x1 -> x0, other arithmetic: 0.69 us -> none  [by_kernel(): return jnp.sum(parts, axis=0)]
    unnamed x0 -> x1, local copies, waits for them, and re-layouts: none -> 0.66 us
    pallas_call x1, Pallas kernels: 28.3 us -> 27.9 us  [by_kernel(): pl.pallas_call(kernel, out_shape=pltpu.VMEM((rows, columns), jnp.float32)...]
where the time goes in v5:
time: 28.7 us; the launch traced here: 28.6 us
  Pallas kernels  27.9 us (97%)
  local copies, waits for them, and re-layouts  0.66 us (2%)
    pallas_call x1, Pallas kernels, by_kernel(): pl.pallas_call(kernel, out_shape=pltpu.VMEM((rows, columns), jnp.float32)...  27.9 us
    unnamed x1, local copies, waits for them, and re-layouts  0.66 us

profile of v5, /device:TPU:1, one launch (start us, length us, event | category | flops | bytes accessed | tf_op | source)
XLA Modules:
  0.0 28.6 jit_solution(12535611016286034446)
XLA Ops:
  0.0 27.9 %shard_map.28 = f32[64,512]{1,0:T(8,128)S(1)} custom-call(bf16[64,8,200]{2,1,0:T(8,128)(2,1)} %amp_ref.1, bf16[800,512]{1,0:T(8,128)(2,1)} %bitcast.1), custom_call_target="tpu_custom_call" | custom-call | tf_op jit(solution)/shard_map/pallas_call | solution.py:237
  27.9 0.7 %copy.4 = f32[64,512]{1,0:T(8,128)} copy(f32[64,512]{1,0:T(8,128)S(1)} %shard_map.28) | data formatting | bytes 262144
